TPU v7x, 32 devices: a whole 2x2x4 slice. The times are simulated.
32 devices in a mesh: dp: 2 (over core), ctx: 8 (over z, y), fsdp: 2 (over x).
Axes of the slice: x: 2, y: 2, z: 4, core: 2. Of those that a mesh axis runs over, the one named last changes fastest.
Arguments:
- tokens: bfloat16 [4, 1024, 1152], P(('dp', 'fsdp'), 'ctx'), may hold values from -6 to 6
- cotangent: bfloat16 [4, 1024, 1152], P(('dp', 'fsdp'), 'ctx'), may hold values from -6 to 6
- segments: int32 [4, 1024], P(('dp', 'fsdp')), may hold values from 0 to 15, never falling along the last dimension, each value on 1 to 640 neighbouring positions
- qkv_weight: float32 [1536, 1152], P(('ctx', 'fsdp')), may hold values from -0.1875 to 0.1875
- out_weight: float32 [1024, 1152], P(('ctx', 'fsdp')), may hold values from -0.1875 to 0.1875
- gate_up_weight: float32 [13824, 1152], P(('ctx', 'fsdp')), may hold values from -0.1875 to 0.1875
- down_weight: float32 [6912, 1152], P(('ctx', 'fsdp')), may hold values from -0.078125 to 0.078125
- gains: float32 [5120], P(('ctx', 'fsdp')), may hold values from -0.15 to 0.15
- qkv_first: float32 [1536, 1152], P(('ctx', 'fsdp')), may hold values from -90 to 90
- out_first: float32 [1024, 1152], P(('ctx', 'fsdp')), may hold values from -90 to 90
- gate_up_first: float32 [13824, 1152], P(('ctx', 'fsdp')), may hold values from -90 to 90
- down_first: float32 [6912, 1152], P(('ctx', 'fsdp')), may hold values from -90 to 90
- gains_first: float32 [5120], P(('ctx', 'fsdp')), may hold values from -90 to 90
- qkv_second: float32 [1536, 1152], P(('ctx', 'fsdp')), may hold values from 300 to 3000
- out_second: float32 [1024, 1152], P(('ctx', 'fsdp')), may hold values from 300 to 3000
- gate_up_second: float32 [13824, 1152], P(('ctx', 'fsdp')), may hold values from 300 to 3000
- down_second: float32 [6912, 1152], P(('ctx', 'fsdp')), may hold values from 300 to 3000
- gains_second: float32 [5120], P(('ctx', 'fsdp')), may hold values from 300 to 3000
Outputs:
- output: bfloat16 [4, 1024, 1152], P(('dp', 'fsdp'), 'ctx')
- input_grad: float32 [4, 1024, 1152], P(('dp', 'fsdp'), 'ctx')
- qkv_grad: float32 [1536, 1152], P(('ctx', 'fsdp'))
- out_grad: float32 [1024, 1152], P(('ctx', 'fsdp'))
- gate_up_grad: float32 [13824, 1152], P(('ctx', 'fsdp'))
- down_grad: float32 [6912, 1152], P(('ctx', 'fsdp'))
- gains_grad: float32 [5120], P(('ctx', 'fsdp'))
- qkv_new: float32 [1536, 1152], P(('ctx', 'fsdp'))
- out_new: float32 [1024, 1152], P(('ctx', 'fsdp'))
- gate_up_new: float32 [13824, 1152], P(('ctx', 'fsdp'))
- down_new: float32 [6912, 1152], P(('ctx', 'fsdp'))
- gains_new: float32 [5120], P(('ctx', 'fsdp'))
- qkv_first_new: float32 [1536, 1152], P(('ctx', 'fsdp'))
- out_first_new: float32 [1024, 1152], P(('ctx', 'fsdp'))
- gate_up_first_new: float32 [13824, 1152], P(('ctx', 'fsdp'))
- down_first_new: float32 [6912, 1152], P(('ctx', 'fsdp'))
- gains_first_new: float32 [5120], P(('ctx', 'fsdp'))
- qkv_second_new: float32 [1536, 1152], P(('ctx', 'fsdp'))
- out_second_new: float32 [1024, 1152], P(('ctx', 'fsdp'))
- gate_up_second_new: float32 [13824, 1152], P(('ctx', 'fsdp'))
- down_second_new: float32 [6912, 1152], P(('ctx', 'fsdp'))
- gains_second_new: float32 [5120], P(('ctx', 'fsdp'))
Inputs may be any that keep to these rules, and one draw needn't show every extreme that they name: `segments`: in each sequence the segment numbers never fall, every number appears, each document has 1 to 640 tokens, and one has exactly 640.
All inputs are finite; a program needn't handle non-finite values.
Results may differ from a plain program's by a relative error of at most 0.018.
Values may be sent and summed in bfloat16 or wider, within the bound.
A program may use at most 320 MiB of HBM per device.

v0:
```python
import jax
import jax.numpy as jnp
from jax import lax
from jax.sharding import PartitionSpec as P

H = 4
HD = 256
STEP = 5


def normalize(value, gain):
    scale = lax.rsqrt(jnp.mean(value * value, axis=-1, keepdims=True) + 1e-06)
    return value * scale * (1.0 + gain)


def rotate(value, angles):
    half = value.shape[-1] // 2
    first = value[..., :half]
    second = value[..., half:]
    cosine = jnp.cos(angles)
    sine = jnp.sin(angles)
    return jnp.concatenate(
        [first * cosine - second * sine, second * cosine + first * sine], axis=-1
    )


def rope_angles(segments):
    count = segments.shape[0]
    index = jnp.arange(count, dtype=jnp.int32)
    change = jnp.concatenate([jnp.ones((1,), dtype=jnp.bool_), segments[1:] != segments[:-1]])
    starts = lax.cummax(jnp.where(change, index, 0), axis=0)
    offset = (index - starts).astype(jnp.float32)
    inverse = jnp.exp(-jnp.log(1000000.0) * (2.0 * jnp.arange(HD // 2, dtype=jnp.float32)) / HD)
    return offset[:, None] * inverse[None, :]


def contract_last(left, right):
    return lax.dot_general(
        left, right, (((1,), (1,)), ((), ())), preferred_element_type=jnp.float32
    )


def contract_first(left, right):
    return lax.dot_general(
        left, right, (((0,), (0,)), ((), ())), preferred_element_type=jnp.float32
    )


def activate(gate_up):
    half = gate_up.shape[-1] // 2
    return jax.nn.gelu(gate_up[:, :half], approximate=True) * gate_up[:, half:]


def adamw(weight, grad, first, second):
    first_new = 0.9 * first + 0.1 * grad
    second_new = 0.95 * second + 0.05 * grad * grad
    first_hat = first_new / (1.0 - 0.9**STEP)
    second_hat = second_new / (1.0 - 0.95**STEP)
    weight_new = weight - 0.03 * (first_hat / (jnp.sqrt(second_hat) + 1e-08) + 0.1 * weight)
    return (weight_new, first_new, second_new)


def body(
    tokens,
    cotangent,
    segments,
    qkv_weight,
    out_weight,
    gate_up_weight,
    down_weight,
    gains,
    qkv_first,
    out_first,
    gate_up_first,
    down_first,
    gains_first,
    qkv_second,
    out_second,
    gate_up_second,
    down_second,
    gains_second,
):
    rows = tokens.shape[1]
    width = tokens.shape[2]
    length = segments.shape[1]
    query_width = H * HD
    scale = HD ** (-0.5)
    reach = lax.axis_size("ctx") // 2 + 1
    front = reach * rows
    window = front + rows
    qkv_full, out_full, gains_full = (
        lax.all_gather(qkv_weight.astype(jnp.bfloat16), ("ctx", "fsdp"), axis=0, tiled=True),
        lax.all_gather(out_weight.astype(jnp.bfloat16), ("ctx", "fsdp"), axis=0, tiled=True),
        lax.all_gather(gains.astype(jnp.bfloat16), ("ctx", "fsdp"), axis=0, tiled=True),
    )
    gain_all = gains_full.astype(jnp.float32)
    gain_input = gain_all[:width]
    gain_attend = gain_all[width : 2 * width]
    gain_pre = gain_all[2 * width : 3 * width]
    gain_post = gain_all[3 * width : 4 * width]
    gain_query = gain_all[4 * width : 4 * width + HD]
    gain_key = gain_all[4 * width + HD :]
    first_row = lax.axis_index("ctx") * rows
    sequence_ids = segments[0]
    angles = lax.dynamic_slice_in_dim(rope_angles(sequence_ids), first_row, rows, 0)
    query_ids = lax.dynamic_slice_in_dim(sequence_ids, first_row, rows, 0)
    query_pos = first_row + jnp.arange(rows, dtype=jnp.int32)
    window_pos = first_row - front + jnp.arange(window, dtype=jnp.int32)
    padded_ids = jnp.concatenate([jnp.full((front,), -1, dtype=jnp.int32), sequence_ids])
    window_ids = lax.dynamic_slice_in_dim(padded_ids, first_row, window, 0)
    allowed = (window_pos[None, :] <= query_pos[:, None]) & (
        window_ids[None, :] == query_ids[:, None]
    )
    allowed = allowed[:, None, :]
    x_rows = tokens[0].astype(jnp.float32)
    normed, input_back = jax.vjp(normalize, x_rows, gain_input)
    normed_low = normed.astype(jnp.bfloat16)
    projected = contract_last(normed_low, qkv_full)
    proj_query = projected[:, :query_width].reshape(rows, H, HD)
    proj_key = projected[:, query_width : query_width + HD]
    proj_value = projected[:, query_width + HD :]

    def query_key(part_query, part_key, query_gain, key_gain):
        return (
            rotate(normalize(part_query, query_gain), angles[:, None, :]),
            rotate(normalize(part_key, key_gain), angles),
        )

    (rotated_query, rotated_key), rotate_back = jax.vjp(
        query_key, proj_query, proj_key, gain_query, gain_key
    )
    query = rotated_query.astype(jnp.bfloat16)
    key_low = rotated_key.astype(jnp.bfloat16)
    value_low = proj_value.astype(jnp.bfloat16)
    keys_all, values_all = (
        lax.all_gather(key_low, "ctx", axis=0, tiled=True),
        lax.all_gather(value_low, "ctx", axis=0, tiled=True),
    )
    blank = jnp.zeros((front, HD), jnp.bfloat16)
    keys = lax.dynamic_slice_in_dim(jnp.concatenate([blank, keys_all]), first_row, window, 0)
    values = lax.dynamic_slice_in_dim(jnp.concatenate([blank, values_all]), first_row, window, 0)
    scores = jnp.einsum("thd,ld->thl", query, keys, preferred_element_type=jnp.float32) * scale
    masked = jnp.where(allowed, scores, -1e30)
    largest = jnp.max(masked, axis=-1, keepdims=True)
    log_total = largest + jnp.log(jnp.sum(jnp.exp(masked - largest), axis=-1, keepdims=True))
    probs_low = jnp.exp(masked - log_total).astype(jnp.bfloat16)
    attended = jnp.einsum("thl,ld->thd", probs_low, values, preferred_element_type=jnp.float32)
    attended = attended.reshape(rows, query_width).astype(jnp.bfloat16)
    branch = jnp.dot(attended, out_full, preferred_element_type=jnp.float32)
    branch_normed, attend_back = jax.vjp(normalize, branch, gain_attend)
    hidden = x_rows + branch_normed
    gate_up_full, down_full = (
        lax.all_gather(gate_up_weight.astype(jnp.bfloat16), ("ctx", "fsdp"), axis=0, tiled=True),
        lax.all_gather(down_weight.astype(jnp.bfloat16), ("ctx", "fsdp"), axis=0, tiled=True),
    )
    hidden_normed, pre_back = jax.vjp(normalize, hidden, gain_pre)
    hidden_low = hidden_normed.astype(jnp.bfloat16)
    gate_up = contract_last(hidden_low, gate_up_full)
    mixed, mix_back = jax.vjp(activate, gate_up)
    mixed_low = mixed.astype(jnp.bfloat16)
    down = jnp.dot(mixed_low, down_full, preferred_element_type=jnp.float32)
    down_normed, post_back = jax.vjp(normalize, down, gain_post)
    output = (hidden + down_normed).astype(jnp.bfloat16)
    gate_up_back, down_back = (
        lax.all_gather(gate_up_weight.astype(jnp.bfloat16), ("ctx", "fsdp"), axis=0, tiled=True),
        lax.all_gather(down_weight.astype(jnp.bfloat16), ("ctx", "fsdp"), axis=0, tiled=True),
    )
    grad_rows = cotangent[0].astype(jnp.float32)
    grad_down, grad_gain_post = post_back(grad_rows)
    grad_down_low = grad_down.astype(jnp.bfloat16)
    down_grad = contract_first(mixed_low, grad_down_low)
    grad_mixed = contract_last(grad_down_low, down_back)
    (grad_gate_up,) = mix_back(grad_mixed)
    grad_gate_up_low = grad_gate_up.astype(jnp.bfloat16)
    gate_up_grad = contract_first(grad_gate_up_low, hidden_low)
    grad_hidden_low = jnp.dot(grad_gate_up_low, gate_up_back, preferred_element_type=jnp.float32)
    grad_from_pre, grad_gain_pre = pre_back(grad_hidden_low)
    grad_hidden = grad_rows + grad_from_pre
    gate_up_part, down_part = (
        lax.psum_scatter(gate_up_grad, ("ctx", "fsdp"), scatter_dimension=0, tiled=True),
        lax.psum_scatter(down_grad, ("ctx", "fsdp"), scatter_dimension=0, tiled=True),
    )
    qkv_back, out_back = (
        lax.all_gather(qkv_weight.astype(jnp.bfloat16), ("ctx", "fsdp"), axis=0, tiled=True),
        lax.all_gather(out_weight.astype(jnp.bfloat16), ("ctx", "fsdp"), axis=0, tiled=True),
    )
    grad_branch, grad_gain_attend = attend_back(grad_hidden)
    grad_branch_low = grad_branch.astype(jnp.bfloat16)
    out_grad = contract_first(attended, grad_branch_low)
    grad_attended = (
        contract_last(grad_branch_low, out_back).astype(jnp.bfloat16).reshape(rows, H, HD)
    )
    scores_again = (
        jnp.einsum("thd,ld->thl", query, keys, preferred_element_type=jnp.float32) * scale
    )
    probs = jnp.exp(jnp.where(allowed, scores_again, -1e30) - log_total)
    grad_probs = jnp.einsum(
        "thd,ld->thl", grad_attended, values, preferred_element_type=jnp.float32
    )
    row_term = jnp.sum(probs * grad_probs, axis=-1, keepdims=True)
    grad_scores = (probs * (grad_probs - row_term)).astype(jnp.bfloat16)
    grad_query = (
        jnp.einsum("thl,ld->thd", grad_scores, keys, preferred_element_type=jnp.float32) * scale
    )
    grad_keys = (
        jnp.einsum("thl,thd->ld", grad_scores, query, preferred_element_type=jnp.float32) * scale
    )
    grad_values = jnp.einsum(
        "thl,thd->ld", probs.astype(jnp.bfloat16), grad_attended, preferred_element_type=jnp.float32
    )
    empty = jnp.zeros((front + length, HD), jnp.float32)
    keys_spread = lax.dynamic_update_slice_in_dim(empty, grad_keys, first_row, 0)[front:]
    values_spread = lax.dynamic_update_slice_in_dim(empty, grad_values, first_row, 0)[front:]
    grad_key, grad_value = (
        lax.psum_scatter(keys_spread, "ctx", scatter_dimension=0, tiled=True),
        lax.psum_scatter(values_spread, "ctx", scatter_dimension=0, tiled=True),
    )
    grad_proj_query, grad_proj_key, grad_gain_query, grad_gain_key = rotate_back(
        (grad_query, grad_key)
    )
    grad_projected = jnp.concatenate(
        [grad_proj_query.reshape(rows, query_width), grad_proj_key, grad_value], axis=1
    ).astype(jnp.bfloat16)
    qkv_grad = contract_first(grad_projected, normed_low)
    grad_normed = jnp.dot(grad_projected, qkv_back, preferred_element_type=jnp.float32)
    grad_from_input, grad_gain_input = input_back(grad_normed)
    input_grad = grad_hidden + grad_from_input
    gains_grad = jnp.concatenate(
        [
            grad_gain_input,
            grad_gain_attend,
            grad_gain_pre,
            grad_gain_post,
            grad_gain_query,
            grad_gain_key,
        ]
    )
    qkv_part, out_part, gains_part = (
        lax.psum_scatter(qkv_grad, ("ctx", "fsdp"), scatter_dimension=0, tiled=True),
        lax.psum_scatter(out_grad, ("ctx", "fsdp"), scatter_dimension=0, tiled=True),
        lax.psum_scatter(gains_grad, ("ctx", "fsdp"), scatter_dimension=0, tiled=True),
    )
    qkv_total, out_total, gate_up_total, down_total, gains_total = (
        lax.psum(qkv_part.astype(jnp.bfloat16), "dp").astype(jnp.float32),
        lax.psum(out_part.astype(jnp.bfloat16), "dp").astype(jnp.float32),
        lax.psum(gate_up_part.astype(jnp.bfloat16), "dp").astype(jnp.float32),
        lax.psum(down_part.astype(jnp.bfloat16), "dp").astype(jnp.float32),
        lax.psum(gains_part.astype(jnp.bfloat16), "dp").astype(jnp.float32),
    )
    qkv_new, qkv_first_new, qkv_second_new = adamw(qkv_weight, qkv_total, qkv_first, qkv_second)
    out_new, out_first_new, out_second_new = adamw(out_weight, out_total, out_first, out_second)
    gate_up_new, gate_up_first_new, gate_up_second_new = adamw(
        gate_up_weight, gate_up_total, gate_up_first, gate_up_second
    )
    down_new, down_first_new, down_second_new = adamw(
        down_weight, down_total, down_first, down_second
    )
    gains_new, gains_first_new, gains_second_new = adamw(
        gains, gains_total, gains_first, gains_second
    )
    return (
        output[None],
        input_grad[None],
        qkv_total,
        out_total,
        gate_up_total,
        down_total,
        gains_total,
        qkv_new,
        out_new,
        gate_up_new,
        down_new,
        gains_new,
        qkv_first_new,
        out_first_new,
        gate_up_first_new,
        down_first_new,
        gains_first_new,
        qkv_second_new,
        out_second_new,
        gate_up_second_new,
        down_second_new,
        gains_second_new,
    )


def solution(mesh):
    in_specs = (
        P(("dp", "fsdp"), "ctx", None),
        P(("dp", "fsdp"), "ctx", None),
        P(("dp", "fsdp"), None),
        P(("ctx", "fsdp"), None),
        P(("ctx", "fsdp"), None),
        P(("ctx", "fsdp"), None),
        P(("ctx", "fsdp"), None),
        P(("ctx", "fsdp")),
        P(("ctx", "fsdp"), None),
        P(("ctx", "fsdp"), None),
        P(("ctx", "fsdp"), None),
        P(("ctx", "fsdp"), None),
        P(("ctx", "fsdp")),
        P(("ctx", "fsdp"), None),
        P(("ctx", "fsdp"), None),
        P(("ctx", "fsdp"), None),
        P(("ctx", "fsdp"), None),
        P(("ctx", "fsdp")),
    )
    out_specs = (
        P(("dp", "fsdp"), "ctx", None),
        P(("dp", "fsdp"), "ctx", None),
        P(("ctx", "fsdp"), None),
        P(("ctx", "fsdp"), None),
        P(("ctx", "fsdp"), None),
        P(("ctx", "fsdp"), None),
        P(("ctx", "fsdp")),
        P(("ctx", "fsdp"), None),
        P(("ctx", "fsdp"), None),
        P(("ctx", "fsdp"), None),
        P(("ctx", "fsdp"), None),
        P(("ctx", "fsdp")),
        P(("ctx", "fsdp"), None),
        P(("ctx", "fsdp"), None),
        P(("ctx", "fsdp"), None),
        P(("ctx", "fsdp"), None),
        P(("ctx", "fsdp")),
        P(("ctx", "fsdp"), None),
        P(("ctx", "fsdp"), None),
        P(("ctx", "fsdp"), None),
        P(("ctx", "fsdp"), None),
        P(("ctx", "fsdp")),
    )
    return jax.shard_map(body, mesh=mesh, in_specs=in_specs, out_specs=out_specs, check_vma=False)
```

profile of v0, /device:TPU:0, one launch (start us, length us, event | category | flops | bytes accessed | tf_op | source)
XLA Modules:
  0.0 2683.0 jit_solution(189627027710603914)
XLA Ops:
  10.8 3.7 convert_element_type.124
  17.3 79.4 %all-reduce.9 = bf16[5120]{0:T(1024)(128)(2,1)S(1)} all-reduce(bf16[5120]{0:T(1024)(128)(2,1)S(1)} %dynamic-update-slice), channel_id=1, replica_groups=mesh['dp'=2,'ctx'=8,'fsdp'=2] {'ctx','fsdp'}, use_global_device_ids=true, to_apply=%add.9 | all-reduce | flops 5120 | bytes 20480
  103.2 31.8 %all_gather.27 = bf16[1024,256]{1,0:T(8,128)(2,1)S(1)} all-gather(bf16[128,256]{1,0:T(8,128)(2,1)S(1)} %pad_maximum_fusion.6), channel_id=1, replica_groups=mesh['dp'=2,'ctx'=8,'fsdp'=2] {'ctx'}, dimensions={0}, use_global_device_ids=true | all-gather | bytes 589824 | tf_op jit(solution)/shard_map/all_gather | solution.py:136
  137.5 32.5 %all_gather.28 = bf16[1024,256]{1,0:T(8,128)(2,1)S(1)} all-gather(bf16[128,256]{1,0:T(8,128)(2,1)S(1)} %slice.142), channel_id=1, replica_groups=mesh['dp'=2,'ctx'=8,'fsdp'=2] {'ctx'}, dimensions={0}, use_global_device_ids=true | all-gather | bytes 589824 | tf_op jit(solution)/shard_map/all_gather | solution.py:137
  173.6 318.3 %all-gather.9.cloned.1.call-done = bf16[13824,1152]{1,0:T(8,128)(2,1)} async-done(((bf16[864,1152]{1,0:T(8,128)(2,1)}), bf16[13824,1152]{1,0:T(8,128)(2,1)}) %all-gather.9.cloned.1.call-update) | async-done | bytes 31850512 | tf_op jit(solution)/shard_map/all_gather | solution.py:153
  491.9 18.4 fusion.91
  510.3 4.3 multiply_convert_fusion
  514.6 162.3 %all-gather.11.cloned.1.call-done = bf16[6912,1152]{1,0:T(8,128)(2,1)} async-done(((bf16[432,1152]{1,0:T(8,128)(2,1)}), bf16[6912,1152]{1,0:T(8,128)(2,1)}) %all-gather.11.cloned.1.call-update) | async-done | bytes 15925264 | tf_op jit(solution)/shard_map/all_gather | solution.py:154
  677.0 8.1 multiply_reduce_fusion.5
  686.9 12.4 fusion.11
  699.3 18.4 multiply_reduce_fusion.1
  735.7 51.3 %reduce-scatter.9.cloned.1.call-done = f32[128,256]{1,0:T(8,128)} async-done(((f32[1024,256]{1,0:T(8,128)}), f32[128,256]{1,0:T(8,128)}) %reduce-scatter.9.cloned.1.call-update) | async-done | bytes 131088 | tf_op jit(solution)/shard_map/reduce_scatter | solution.py:216
  788.0 65.7 %reduce-scatter.7.cloned.1.call-done = f32[128,256]{1,0:T(8,128)} async-done(((f32[1024,256]{1,0:T(8,128)}), f32[128,256]{1,0:T(8,128)}) %reduce-scatter.7.cloned.1.call-update) | async-done | bytes 131088 | tf_op jit(solution)/shard_map/reduce_scatter | solution.py:215
  858.4 4.0 fusion.48
  863.4 12.9 fusion.100
  877.4 26.9 %fusion.29 = f32[13824,1152]{1,0:T(8,128)} fusion(f32[128,6912]{1,0:T(8,128)} %get-tuple-element.62, f32[128,6912]{1,0:T(8,128)} %get-tuple-element.61, f32[128,1152]{1,0:T(8,128)S(1)} %copy-done.2, f32[1152]{0:T(1024)S(1)} %get-tuple-element.74, f32[128]{0:T(128)S(1)} %fusion.79), kind=kOutput, calls=%fused_computation.81 | convolution fusion | flops 4080844800 | bytes 71373824 | tf_op jit(solution)/shard_map/dot_general | solution.py:44
  904.3 91.1 %reduce-scatter.13.cloned.1.call-done = f32[64,1152]{1,0:T(8,128)} async-done(((f32[1024,1152]{1,0:T(8,128)}), f32[64,1152]{1,0:T(8,128)}) %reduce-scatter.13.cloned.1.call-update) | async-done | bytes 294928 | tf_op jit(solution)/shard_map/reduce_scatter | solution.py:240
  997.1 154.8 %reduce-scatter.11.cloned.1.call-done = f32[96,1152]{1,0:T(8,128)} async-done(((f32[1536,1152]{1,0:T(8,128)}), f32[96,1152]{1,0:T(8,128)}) %reduce-scatter.11.cloned.1.call-update) | async-done | bytes 442384 | tf_op jit(solution)/shard_map/reduce_scatter | solution.py:239
  1153.7 483.3 %reduce-scatter.17.cloned.1.call-done = f32[432,1152]{1,0:T(8,128)} async-done(((f32[6912,1152]{1,0:T(8,128)}), f32[432,1152]{1,0:T(8,128)}) %reduce-scatter.17.cloned.1.call-update) | async-done | bytes 1990672 | tf_op jit(solution)/shard_map/reduce_scatter | solution.py:181
  1639.6 920.1 %reduce-scatter.15.cloned.1.call-done = f32[864,1152]{1,0:T(8,128)} async-done(((f32[13824,1152]{1,0:T(8,128)}), f32[864,1152]{1,0:T(8,128)}) %reduce-scatter.15.cloned.1.call-update) | async-done | bytes 3981328 | tf_op jit(solution)/shard_map/reduce_scatter | solution.py:180
  2559.7 3.6 convert_element_type.139
  2575.2 75.5 %all-reduce.10 = bf16[5120]{0:T(1024)(128)(2,1)S(1)} all-reduce(f32[5120]{0:T(1024)} %constant_dynamic-update-slice_fusion), channel_id=8, replica_groups=mesh['dp'=2,'ctx'=8,'fsdp'=2] {'ctx','fsdp'}, use_global_device_ids=true, to_apply=%region_33.34.clone | all-reduce | flops 5120 | bytes 30720
  2662.3 10.2 multiply_subtract_fusion
  2672.6 3.6 multiply_subtract_fusion.1
  (240 shorter events, 73.7 us)
Async XLA Ops:
  7.2 91.5 %all-gather.5.cloned.1.call-start = ((), (), s32[]{:S(2)}) async-start(), calls=%async_computation.6 | async-start | bytes 3760128 | tf_op jit(solution)/shard_map/all_gather | solution.py:92
  9.0 161.9 %all-gather.7.cloned.1.call-start = ((), (), s32[]{:S(2)}) async-start(), calls=%async_computation.7 | async-start | bytes 2506752 | tf_op jit(solution)/shard_map/all_gather | solution.py:93
  10.7 481.2 %all-gather.9.cloned.1.call-start = ((), (), s32[]{:S(2)}) async-start(), calls=%async_computation.8 | async-start | bytes 33841152 | tf_op jit(solution)/shard_map/all_gather | solution.py:153
  14.5 82.2 %copy-start.40 = (s32[1,1024]{1,0:T(1,128)S(1)}, s32[1,1024]{1,0:T(1,128)}, u32[]{:S(2)}) copy-start(s32[1,1024]{1,0:T(1,128)} %param.20) | copy-start | bytes 12292
  14.5 83.1 %copy-start.7 = (bf16[1,128,1152]{2,1,0:T(8,128)(2,1)S(1)}, bf16[1,128,1152]{2,1,0:T(8,128)(2,1)}, u32[]{:S(2)}) copy-start(bf16[1,128,1152]{2,1,0:T(8,128)(2,1)} %param.18) | copy-start | bytes 884740
  14.5 662.4 %all-gather.11.cloned.1.call-start = ((), (), s32[]{:S(2)}) async-start(), calls=%async_computation.9 | async-start | bytes 16920576 | tf_op jit(solution)/shard_map/all_gather | solution.py:154
  15.7 771.3 %reduce-scatter.9.cloned.1.call-start = ((), (), s32[]{:S(2)}) async-start(), calls=%async_computation.11 | async-start | bytes 1179648 | tf_op jit(solution)/shard_map/reduce_scatter | solution.py:216
  170.9 321.0 %copy-start.22 = (bf16[128,4,256]{0,2,1:T(8,128)(2,1)}, bf16[128,4,256]{0,2,1:T(8,128)(2,1)S(1)}, u32[]{:S(2)}) copy-start(bf16[128,4,256]{0,2,1:T(8,128)(2,1)S(1)} %copy.88) | copy-start | bytes 786436
  173.3 318.6 %copy-start.10 = (f32[128,1152]{1,0:T(8,128)}, f32[128,1152]{1,0:T(8,128)S(1)}, u32[]{:S(2)}) copy-start(f32[128,1152]{1,0:T(8,128)S(1)} %get-tuple-element.86) | copy-start | bytes 1769476
  173.6 318.3 %copy-start = (f32[128,1152]{1,0:T(8,128)}, f32[128,1152]{1,0:T(8,128)S(1)}, u32[]{:S(2)}) copy-start(f32[128,1152]{1,0:T(8,128)S(1)} %get-tuple-element.60) | copy-start | bytes 1769476
  725.2 128.5 %reduce-scatter.7.cloned.1.call-start = ((), (), s32[]{:S(2)}) async-start(), calls=%async_computation.10 | async-start | bytes 1179648 | tf_op jit(solution)/shard_map/reduce_scatter | solution.py:215
  729.2 266.3 %reduce-scatter.13.cloned.1.call-start = ((), (), s32[]{:S(2)}) async-start(), calls=%async_computation.13 | async-start | bytes 5013504 | tf_op jit(solution)/shard_map/reduce_scatter | solution.py:240
  732.1 122.8 %copy-start.45 = (f32[256]{0:T(256)S(1)}, f32[256]{0:T(256)}, u32[]{:S(2)}) copy-start(f32[256]{0:T(256)} %copy-done.44) | copy-start | bytes 3076
  732.2 126.2 %copy-start.8 = (bf16[1,128,1152]{2,1,0:T(8,128)(2,1)S(1)}, bf16[1,128,1152]{2,1,0:T(8,128)(2,1)}, u32[]{:S(2)}) copy-start(bf16[1,128,1152]{2,1,0:T(8,128)(2,1)} %param.18) | copy-start | bytes 884740
  732.2 126.2 %copy-start.50 = (f32[128]{0:T(128)S(1)}, f32[128]{0:T(128)}, u32[]{:S(2)}) copy-start(f32[128]{0:T(128)} %copy-done.49) | copy-start | bytes 1540
  732.2 419.8 %reduce-scatter.11.cloned.1.call-start = ((), (), s32[]{:S(2)}) async-start(), calls=%async_computation.12 | async-start | bytes 7520256 | tf_op jit(solution)/shard_map/reduce_scatter | solution.py:239
  735.7 126.7 %copy-start.24 = (bf16[128,4,256]{0,2,1:T(8,128)(2,1)}, bf16[128,4,256]{0,2,1:T(8,128)(2,1)S(1)}, u32[]{:S(2)}) copy-start(bf16[128,4,256]{0,2,1:T(8,128)(2,1)S(1)} %copy.92) | copy-start | bytes 786436
  862.4 774.5 %reduce-scatter.17.cloned.1.call-start = ((), (), s32[]{:S(2)}) async-start(), calls=%async_computation.15 | async-start | bytes 33841152 | tf_op jit(solution)/shard_map/reduce_scatter | solution.py:181
  876.3 1683.4 %reduce-scatter.15.cloned.1.call-start = ((), (), s32[]{:S(2)}) async-start(), calls=%async_computation.14 | async-start | bytes 67682304 | tf_op jit(solution)/shard_map/reduce_scatter | solution.py:180
  904.3 1753.2 %all-reduce.14.cloned.1.call-start = ((), (), s32[]{:S(2)}) async-start(), calls=%async_computation.16 | async-start | bytes 6709248 | tf_op jit(solution)/shard_map/psum | solution.py:244
  1639.6 924.4 %copy-start.4 = (bf16[1536,1152]{1,0:T(8,128)(2,1)S(1)}, bf16[1536,1152]{1,0:T(8,128)(2,1)}, u32[]{:S(2)}) copy-start(bf16[1536,1152]{1,0:T(8,128)(2,1)} %all-gather.5.cloned.1.call-done) | copy-start | bytes 10616836
  2567.3 93.0 %copy-start.28 = (f32[64,1152]{1,0:T(8,128)S(1)}, f32[64,1152]{1,0:T(8,128)}, u32[]{:S(2)}) copy-start(f32[64,1152]{1,0:T(8,128)} %param.22) | copy-start | bytes 884740
  2567.3 93.0 %copy-start.34 = (f32[64,1152]{1,0:T(8,128)S(1)}, f32[64,1152]{1,0:T(8,128)}, u32[]{:S(2)}) copy-start(f32[64,1152]{1,0:T(8,128)} %param.27) | copy-start | bytes 884740
  2567.3 93.0 %copy-start.35 = (f32[64,1152]{1,0:T(8,128)S(1)}, f32[64,1152]{1,0:T(8,128)}, u32[]{:S(2)}) copy-start(f32[64,1152]{1,0:T(8,128)} %param.32) | copy-start | bytes 884740
  (46 other events, 426.2 us)
Sparse Core Ops, SparseCore 0:
  11.4 74.5 all-gather.4
  89.4 64.6 all-gather.6
  157.5 334.3 all-gather.8
  495.1 181.8 all-gather.10
  725.3 61.6 reduce-scatter.8
  791.2 62.4 reduce-scatter.6
  858.9 136.5 reduce-scatter.12
  1001.7 150.2 reduce-scatter.10
  1159.0 477.8 reduce-scatter.16
  1643.9 915.7 reduce-scatter.14
  2564.0 23.4 all-reduce.13
where the time goes:
time: 2690 us; the launch traced here: 2680 us
  waiting for transfers between devices  2250 us (84%)
  blocking collectives  222 us (8%)
  matrix products  120 us (4%)
  other arithmetic  60.8 us (2%)
    reduce_scatter x1, waiting for transfers between devices, body(): lax.psum_scatter(gate_up_grad, ('ctx', 'fsdp'), scatter_dimension=0, tile...  920 us
    reduce_scatter x1, waiting for transfers between devices, body(): lax.psum_scatter(down_grad, ('ctx', 'fsdp'), scatter_dimension=0, tiled=T...  483 us
    all_gather x1, waiting for transfers between devices, body(): lax.all_gather(gate_up_weight.astype(jnp.bfloat16), ('ctx', 'fsdp'), axis...  318 us
    all_gather x1, waiting for transfers between devices, body(): lax.all_gather(down_weight.astype(jnp.bfloat16), ('ctx', 'fsdp'), axis=0,...  162 us
    unnamed x2, blocking collectives  155 us
    reduce_scatter x1, waiting for transfers between devices, body(): lax.psum_scatter(qkv_grad, ('ctx', 'fsdp'), scatter_dimension=0, tiled=True)  155 us
    reduce_scatter x1, waiting for transfers between devices, body(): lax.psum_scatter(out_grad, ('ctx', 'fsdp'), scatter_dimension=0, tiled=True)  91.1 us
    reduce_scatter x1, waiting for transfers between devices, body(): lax.psum_scatter(keys_spread, 'ctx', scatter_dimension=0, tiled=True)  65.7 us
  transfers between devices with their start and end apart: 11, of which 8 were waited for; matrix products, arithmetic and copies ran while one was open for 5% of the time, Pallas kernels for 0%

commit v1 on v0

--- a/solution.py
+++ b/solution.py
@@ -6,6 +6,18 @@
 H = 4
 HD = 256
 STEP = 5
+
+
+def collect(value, axis, dim):
+    ways, here, turn = (lax.axis_size(axis), lax.axis_index(axis), value.shape[dim])
+    line, have = (value, 1)
+    while have < ways:
+        line = jnp.concatenate(
+            [line, lax.ppermute(line, axis, [(d, (d - have) % ways) for d in range(ways)])],
+            axis=dim,
+        )
+        have = 2 * have
+    return jnp.roll(line, here * turn, axis=dim)
 
 
 def normalize(value, gain):
@@ -151,7 +163,7 @@
     hidden = x_rows + branch_normed
     gate_up_full, down_full = (
         lax.all_gather(gate_up_weight.astype(jnp.bfloat16), ("ctx", "fsdp"), axis=0, tiled=True),
-        lax.all_gather(down_weight.astype(jnp.bfloat16), ("ctx", "fsdp"), axis=0, tiled=True),
+        collect(down_weight.astype(jnp.bfloat16), ("ctx", "fsdp"), 0),
     )
     hidden_normed, pre_back = jax.vjp(normalize, hidden, gain_pre)
     hidden_low = hidden_normed.astype(jnp.bfloat16)

time: 2690 us -> 3140 us (1.17)
  blocking collectives: 222 us -> 550 us
  waiting for transfers between devices: 2250 us -> 2310 us
    unnamed x2, blocking collectives: 155 us -> 481 us
    ppermute x0 -> x4, waiting for transfers between devices: none -> 185 us  [collect(): lax.ppermute(line, axis, [(d, (d - have) % ways) for d in range(ways)])]
    all_gather x1, waiting for transfers between devices: 318 us -> 204 us  [body(): lax.all_gather(gate_up_weight.astype(jnp.bfloat16), ('ctx', 'fsdp'), axis...]
  transfers between devices with their start and end apart: 11 -> 15, of which waited for: 8 -> 11; matrix products, arithmetic and copies ran while one was open for 5% -> 6% of each run, Pallas kernels for 0% -> 0%
where the time goes in v1:
time: 3140 us
  waiting for transfers between devices  2310 us (74%)
  blocking collectives  550 us (18%)
  matrix products  123 us (4%)
  other arithmetic  84.1 us (3%)
  local copies, waits for them, and re-layouts  46.4 us (1%)
    reduce_scatter x1, waiting for transfers between devices, body(): lax.psum_scatter(gate_up_grad, ('ctx', 'fsdp'), scatter_dimension=0, tile...  920 us
    reduce_scatter x1, waiting for transfers between devices, body(): lax.psum_scatter(down_grad, ('ctx', 'fsdp'), scatter_dimension=0, tiled=T...  484 us
    unnamed x2, blocking collectives  481 us
    all_gather x1, waiting for transfers between devices, body(): lax.all_gather(gate_up_weight.astype(jnp.bfloat16), ('ctx', 'fsdp'), axis...  204 us
    ppermute x4, waiting for transfers between devices, collect(): lax.ppermute(line, axis, [(d, (d - have) % ways) for d in range(ways)])  185 us
    reduce_scatter x1, waiting for transfers between devices, body(): lax.psum_scatter(qkv_grad, ('ctx', 'fsdp'), scatter_dimension=0, tiled=True)  155 us
    all_gather x1, waiting for transfers between devices, body(): lax.all_gather(down_weight.astype(jnp.bfloat16), ('ctx', 'fsdp'), axis=0,...  149 us
    reduce_scatter x1, waiting for transfers between devices, body(): lax.psum_scatter(out_grad, ('ctx', 'fsdp'), scatter_dimension=0, tiled=True)  95.5 us
  transfers between devices with their start and end apart: 15, of which 11 were waited for; matrix products, arithmetic and copies ran while one was open for 6% of the time, Pallas kernels for 0%

profile of v1, /device:TPU:0, one launch (start us, length us, event | category | flops | bytes accessed | tf_op | source)
XLA Modules:
  0.0 3135.4 jit_solution(9215079062652213112)
XLA Ops:
  23.1 26.3 collective-permute-done
  51.2 52.3 %collective-permute-done.1 = bf16[864,1152]{1,0:T(8,128)(2,1)S(1)} collective-permute-done((bf16[864,1152]{1,0:T(8,128)(2,1)S(1)}, bf16[864,1152]{1,0:T(8,128)(2,1)S(1)}, u32[]{:S(2)}, u32[]{:S(2)}) %collective-permute-start.1) | collective-permute-done | bytes 1990688 | tf_op jit(solution)/shard_map/ppermute | solution.py:16
  109.8 106.1 %collective-permute-done.2 = bf16[1728,1152]{1,0:T(8,128)(2,1)S(1)} collective-permute-done((bf16[1728,1152]{1,0:T(8,128)(2,1)S(1)}, bf16[1728,1152]{1,0:T(8,128)(2,1)S(1)}, u32[]{:S(2)}, u32[]{:S(2)}) %collective-permute-start.2) | collective-permute-done | bytes 3981344 | tf_op jit(solution)/shard_map/ppermute | solution.py:16
  215.9 18.3 pad_maximum_fusion
  235.8 405.6 %all-reduce.9 = bf16[5120]{0:T(1024)(128)(2,1)S(1)} all-reduce(bf16[5120]{0:T(1024)(128)(2,1)S(1)} %dynamic-update-slice), channel_id=1, replica_groups=mesh['dp'=2,'ctx'=8,'fsdp'=2] {'ctx','fsdp'}, use_global_device_ids=true, to_apply=%add.9 | all-reduce | flops 5120 | bytes 20480
  651.7 33.0 %all_gather.26 = bf16[1024,256]{1,0:T(8,128)(2,1)S(1)} all-gather(bf16[128,256]{1,0:T(8,128)(2,1)S(1)} %pad_maximum_fusion.9), channel_id=1, replica_groups=mesh['dp'=2,'ctx'=8,'fsdp'=2] {'ctx'}, dimensions={0}, use_global_device_ids=true | all-gather | bytes 589824 | tf_op jit(solution)/shard_map/all_gather | solution.py:148
  687.2 33.2 %all_gather.27 = bf16[1024,256]{1,0:T(8,128)(2,1)S(1)} all-gather(bf16[128,256]{1,0:T(8,128)(2,1)S(1)} %copy-done.44), channel_id=1, replica_groups=mesh['dp'=2,'ctx'=8,'fsdp'=2] {'ctx'}, dimensions={0}, use_global_device_ids=true | all-gather | bytes 589824 | tf_op jit(solution)/shard_map/all_gather | solution.py:149
  743.2 7.1 constant_dynamic-update-slice_fusion
  750.3 203.9 %all-gather.9.cloned.1.call-done = bf16[13824,1152]{1,0:T(8,128)(2,1)} async-done(((bf16[864,1152]{1,0:T(8,128)(2,1)}), bf16[13824,1152]{1,0:T(8,128)(2,1)}) %all-gather.9.cloned.1.call-update) | async-done | bytes 31850512 | tf_op jit(solution)/shard_map/all_gather | solution.py:165
  954.2 18.7 fusion.94
  977.3 11.4 multiply_reduce_fusion.5
  990.4 148.9 %all-gather.11.cloned.1.call-done = bf16[6912,1152]{1,0:T(8,128)(2,1)} async-done(((bf16[432,1152]{1,0:T(8,128)(2,1)}), bf16[6912,1152]{1,0:T(8,128)(2,1)}) %all-gather.11.cloned.1.call-update) | async-done | bytes 15925264 | tf_op jit(solution)/shard_map/all_gather | solution.py:178
  1139.3 12.4 fusion.13
  1151.8 18.4 multiply_reduce_fusion.1
  1185.7 53.8 %reduce-scatter.7.cloned.1.call-done = f32[128,256]{1,0:T(8,128)} async-done(((f32[1024,256]{1,0:T(8,128)}), f32[128,256]{1,0:T(8,128)}) %reduce-scatter.7.cloned.1.call-update) | async-done | bytes 131088 | tf_op jit(solution)/shard_map/reduce_scatter | solution.py:227
  1243.5 62.8 %reduce-scatter.9.cloned.1.call-done = f32[128,256]{1,0:T(8,128)} async-done(((f32[1024,256]{1,0:T(8,128)}), f32[128,256]{1,0:T(8,128)}) %reduce-scatter.9.cloned.1.call-update) | async-done | bytes 131088 | tf_op jit(solution)/shard_map/reduce_scatter | solution.py:228
  1312.8 12.7 fusion.103
  1325.6 26.7 fusion.31
  1352.4 95.5 %reduce-scatter.13.cloned.1.call-done = f32[64,1152]{1,0:T(8,128)} async-done(((f32[1024,1152]{1,0:T(8,128)}), f32[64,1152]{1,0:T(8,128)}) %reduce-scatter.13.cloned.1.call-update) | async-done | bytes 294928 | tf_op jit(solution)/shard_map/reduce_scatter | solution.py:252
  1449.5 154.6 %reduce-scatter.11.cloned.1.call-done = f32[96,1152]{1,0:T(8,128)} async-done(((f32[1536,1152]{1,0:T(8,128)}), f32[96,1152]{1,0:T(8,128)}) %reduce-scatter.11.cloned.1.call-update) | async-done | bytes 442384 | tf_op jit(solution)/shard_map/reduce_scatter | solution.py:251
  1605.9 483.6 %reduce-scatter.17.cloned.1.call-done = f32[432,1152]{1,0:T(8,128)} async-done(((f32[6912,1152]{1,0:T(8,128)}), f32[432,1152]{1,0:T(8,128)}) %reduce-scatter.17.cloned.1.call-update) | async-done | bytes 1990672 | tf_op jit(solution)/shard_map/reduce_scatter | solution.py:193
  2092.1 920.2 %reduce-scatter.15.cloned.1.call-done = f32[864,1152]{1,0:T(8,128)} async-done(((f32[13824,1152]{1,0:T(8,128)}), f32[864,1152]{1,0:T(8,128)}) %reduce-scatter.15.cloned.1.call-update) | async-done | bytes 3981328 | tf_op jit(solution)/shard_map/reduce_scatter | solution.py:192
  3027.7 75.5 %all-reduce.10 = bf16[5120]{0:T(1024)(128)(2,1)S(1)} all-reduce(f32[5120]{0:T(1024)} %constant_dynamic-update-slice_fusion.12), channel_id=8, replica_groups=mesh['dp'=2,'ctx'=8,'fsdp'=2] {'ctx','fsdp'}, use_global_device_ids=true, to_apply=%region_33.34.clone | all-reduce | flops 5120 | bytes 30720
  3110.1 11.5 multiply_subtract_fusion
  (314 shorter events, 126.3 us)
Async XLA Ops:
  7.2 639.2 %all-gather.5.cloned.1.call-start = ((), (), s32[]{:S(2)}) async-start(), calls=%async_computation.6 | async-start | bytes 3760128 | tf_op jit(solution)/shard_map/all_gather | solution.py:104
  9.0 714.5 %all-gather.7.cloned.1.call-start = ((), (), s32[]{:S(2)}) async-start(), calls=%async_computation.7 | async-start | bytes 2506752 | tf_op jit(solution)/shard_map/all_gather | solution.py:105
  10.7 943.5 %all-gather.9.cloned.1.call-start = ((), (), s32[]{:S(2)}) async-start(), calls=%async_computation.8 | async-start | bytes 33841152 | tf_op jit(solution)/shard_map/all_gather | solution.py:165
  14.5 1124.8 %all-gather.11.cloned.1.call-start = ((), (), s32[]{:S(2)}) async-start(), calls=%async_computation.9 | async-start | bytes 16920576 | tf_op jit(solution)/shard_map/all_gather | solution.py:178
  16.1 1223.4 %reduce-scatter.7.cloned.1.call-start = ((), (), s32[]{:S(2)}) async-start(), calls=%async_computation.10 | async-start | bytes 1179648 | tf_op jit(solution)/shard_map/reduce_scatter | solution.py:227
  16.1 33.3 %collective-permute-start = (bf16[432,1152]{1,0:T(8,128)(2,1)}, bf16[432,1152]{1,0:T(8,128)(2,1)S(1)}, u32[]{:S(2)}, u32[]{:S(2)}) collective-permute-start(bf16[432,1152]{1,0:T(8,128)(2,1)} %get-tuple-element.60), channel_id=1, source_target_pairs={{0,15},{1,0},{2,1},{3,2},{4,3},{5,4},{6,5},{7,6},{8,7},{9,8},{10,9... | collective-permute-start | bytes 2985992 | tf_op jit(solution)/shard_map/ppermute | solution.py:16
  49.4 594.5 %copy-start.6 = (bf16[432,1152]{1,0:T(8,128)(2,1)}, bf16[432,1152]{1,0:T(8,128)(2,1)S(1)}, u32[]{:S(2)}) copy-start(bf16[432,1152]{1,0:T(8,128)(2,1)S(1)} %collective-permute-done) | copy-start | bytes 2985988
  51.2 52.4 %collective-permute-start.1 = (bf16[864,1152]{1,0:T(8,128)(2,1)S(1)}, bf16[864,1152]{1,0:T(8,128)(2,1)S(1)}, u32[]{:S(2)}, u32[]{:S(2)}) collective-permute-start(bf16[864,1152]{1,0:T(8,128)(2,1)S(1)} %pad_maximum_fusion.2), channel_id=1, source_target_pairs={{0,14},{1,15},{2,0},{3,1},{4,2},{5,3},{6,4},{7,5},{8,6},{9,7},{10,... | collective-permute-start | bytes 5971976 | tf_op jit(solution)/shard_map/ppermute | solution.py:16
  109.7 124.5 %copy-start.65 = (f32[320]{0:T(512)S(1)}, f32[320]{0:T(512)}, u32[]{:S(2)}) copy-start(f32[320]{0:T(512)} %param.25) | copy-start | bytes 3844
  109.7 124.5 %copy-start.78 = (u32[32]{0:T(128)S(1)}, u32[32]{0:T(128)}, u32[]{:S(2)}) copy-start(u32[32]{0:T(128)} %constant.188) | copy-start | bytes 388
  109.7 531.7 %copy-start.53 = (s32[1,1024]{1,0:T(1,128)S(1)}, s32[1,1024]{1,0:T(1,128)}, u32[]{:S(2)}) copy-start(s32[1,1024]{1,0:T(1,128)} %param.20) | copy-start | bytes 12292
  109.7 532.7 %copy-start.10 = (bf16[1,128,1152]{2,1,0:T(8,128)(2,1)S(1)}, bf16[1,128,1152]{2,1,0:T(8,128)(2,1)}, u32[]{:S(2)}) copy-start(bf16[1,128,1152]{2,1,0:T(8,128)(2,1)} %param.18) | copy-start | bytes 884740
  109.7 106.2 %collective-permute-start.2 = (bf16[1728,1152]{1,0:T(8,128)(2,1)S(1)}, bf16[1728,1152]{1,0:T(8,128)(2,1)S(1)}, u32[]{:S(2)}, u32[]{:S(2)}) collective-permute-start(bf16[1728,1152]{1,0:T(8,128)(2,1)S(1)} %pad_maximum_fusion.1), channel_id=1, source_target_pairs={{0,12},{1,13},{2,14},{3,15},{4,0},{5,1},{6,2},{7,3},{8,4},{9,5},{1... | collective-permute-start | bytes 11943944 | tf_op jit(solution)/shard_map/ppermute | solution.py:16
  234.2 494.9 %collective-permute-start.3 = (bf16[3456,1152]{1,0:T(8,128)(2,1)}, bf16[3456,1152]{1,0:T(8,128)(2,1)}, u32[]{:S(2)}, u32[]{:S(2)}) collective-permute-start(bf16[3456,1152]{1,0:T(8,128)(2,1)} %pad_maximum_fusion), channel_id=1, source_target_pairs={{0,8},{1,9},{2,10},{3,11},{4,12},{5,13},{6,14},{7,15},{8,0},{9,1},... | collective-permute-start | bytes 23887880 | tf_op jit(solution)/shard_map/ppermute | solution.py:16
  990.4 161.3 %copy-start.33 = (bf16[128,1152]{1,0:T(8,128)(2,1)}, bf16[128,1152]{1,0:T(8,128)(2,1)S(1)}, u32[]{:S(2)}) copy-start(bf16[128,1152]{1,0:T(8,128)(2,1)S(1)} %get-tuple-element.69) | copy-start | bytes 884740
  1177.6 128.6 %reduce-scatter.9.cloned.1.call-start = ((), (), s32[]{:S(2)}) async-start(), calls=%async_computation.11 | async-start | bytes 1179648 | tf_op jit(solution)/shard_map/reduce_scatter | solution.py:228
  1179.5 268.4 %reduce-scatter.13.cloned.1.call-start = ((), (), s32[]{:S(2)}) async-start(), calls=%async_computation.13 | async-start | bytes 5013504 | tf_op jit(solution)/shard_map/reduce_scatter | solution.py:252
  1182.6 124.7 %copy-start.67 = (f32[128]{0:T(128)S(1)}, f32[128]{0:T(128)}, u32[]{:S(2)}) copy-start(f32[128]{0:T(128)} %copy-done.66) | copy-start | bytes 1540
  1182.6 421.6 %reduce-scatter.11.cloned.1.call-start = ((), (), s32[]{:S(2)}) async-start(), calls=%async_computation.12 | async-start | bytes 7520256 | tf_op jit(solution)/shard_map/reduce_scatter | solution.py:251
  1185.7 125.6 %copy-start.26 = (bf16[128,4,256]{0,2,1:T(8,128)(2,1)}, bf16[128,4,256]{0,2,1:T(8,128)(2,1)S(1)}, u32[]{:S(2)}) copy-start(bf16[128,4,256]{0,2,1:T(8,128)(2,1)S(1)} %copy.92) | copy-start | bytes 786436
  1311.4 778.1 %reduce-scatter.17.cloned.1.call-start = ((), (), s32[]{:S(2)}) async-start(), calls=%async_computation.15 | async-start | bytes 33841152 | tf_op jit(solution)/shard_map/reduce_scatter | solution.py:193
  1325.6 1686.7 %reduce-scatter.15.cloned.1.call-start = ((), (), s32[]{:S(2)}) async-start(), calls=%async_computation.14 | async-start | bytes 67682304 | tf_op jit(solution)/shard_map/reduce_scatter | solution.py:192
  1352.4 1757.7 %all-reduce.14.cloned.1.call-start = ((), (), s32[]{:S(2)}) async-start(), calls=%async_computation.16 | async-start | bytes 6709248 | tf_op jit(solution)/shard_map/psum | solution.py:256
  2092.1 924.5 %copy-start.7 = (bf16[1536,1152]{1,0:T(8,128)(2,1)S(1)}, bf16[1536,1152]{1,0:T(8,128)(2,1)}, u32[]{:S(2)}) copy-start(bf16[1536,1152]{1,0:T(8,128)(2,1)} %all-gather.5.cloned.1.call-done) | copy-start | bytes 10616836
  (77 other events, 1256.3 us)
Sparse Core Ops, SparseCore 0:
  11.4 135.8 all-gather.4
  150.6 460.2 all-gather.6
  614.3 339.8 all-gather.8
  957.4 181.8 all-gather.10
  1177.7 61.6 reduce-scatter.6
  1243.7 62.4 reduce-scatter.8
  1311.4 136.4 reduce-scatter.12
  1454.1 150.0 reduce-scatter.10
  1611.3 478.1 reduce-scatter.16
  2096.4 915.8 reduce-scatter.14
  3016.6 23.4 all-reduce.13
